TPU v7x, 128 devices: a whole 4x4x4 slice. The times are simulated.
128 devices in a mesh: dc: 16 (over z, x_lo, core), tp: 8 (over y, x_hi).
Axes of the slice: x: 4 (x_hi: 2, x_lo: 2; x = x_hi * 2 + x_lo), y: 4, z: 4, core: 2. Of those that a mesh axis runs over, the one named last changes fastest.
Arguments:
- query_heads: bfloat16 [3584, 8192], P('dc', 'tp'), may hold values from -10 to 10
- key_heads: bfloat16 [3584, 1024], P('dc', 'tp'), may hold values from -11 to 11
- value_heads: bfloat16 [3584, 1024], P('dc', 'tp'), may hold values from -6 to 6
- out_weight: bfloat16 [8192, 8192], P('tp'), may hold values from -0.0625 to 0.0625
- grad_out: bfloat16 [3584, 8192], P('dc', 'tp'), may hold values from -6 to 6
- span_place: int32 [32], replicated, may hold values from 0 to 31, each once
- sample_lengths: int32 [4], replicated, may hold values from 1 to 1792, 3584 in all
Outputs:
- layer_out: bfloat16 [3584, 8192], P('dc', 'tp')
- grad_queries: bfloat16 [3584, 8192], P('dc', 'tp')
- grad_keys: bfloat16 [3584, 1024], P('dc', 'tp')
- grad_values: bfloat16 [3584, 1024], P('dc', 'tp')
- grad_weight: bfloat16 [8192, 8192], P('tp', 'dc')
Inputs may be any that keep to these rules, and one draw needn't show every extreme that they name: `span_place`: each of 0 to 31 once. `sample_lengths`: the lengths sum to 3584; the longest is exactly 1792.
All inputs are finite; a program needn't handle non-finite values.
Results may differ from a plain program's by a relative error of at most 0.039.
Values may be sent and summed in bfloat16 or wider, within the bound.
A program may use at most 128 MiB of HBM per device.

v0:
```python
import jax
import jax.numpy as jnp
from jax import lax
from jax.sharding import PartitionSpec as P

HEADS = 64
KV_HEADS = 8
HEAD_DIM = 128


negative_fill = -1e30


def token_positions(span_place, total_rows, span_count):
    span_rows = total_rows // span_count
    indices = jnp.arange(total_rows, dtype=jnp.int32)
    matches = (indices // span_rows)[:, None] == jnp.arange(span_count, dtype=jnp.int32)[None, :]
    placed = jnp.sum(jnp.where(matches, span_place[None, :], 0), axis=1)
    return placed * span_rows + indices % span_rows


def sample_ids(positions, sample_lengths):
    bounds = jnp.cumsum(sample_lengths)
    return jnp.sum((positions[:, None] >= bounds[None, :]).astype(jnp.int32), axis=1)


def block_scores(query_four, key_block, query_pos, query_sample, key_pos, key_sample, scaling):
    allowed = (key_sample[None, :] == query_sample[:, None]) & (
        key_pos[None, :] <= query_pos[:, None]
    )
    scores = (
        jnp.einsum("tgrd,ngd->grtn", query_four, key_block, preferred_element_type=jnp.float32)
        * scaling
    )
    scores = jnp.where(allowed[None, None], scores, negative_fill)
    return (scores, allowed)


def on_device(
    query_heads, key_heads, value_heads, out_weight, grad_out, span_place, sample_lengths
):
    shard_count = lax.axis_size("dc")
    shard_index = lax.axis_index("dc")
    local_rows = query_heads.shape[0]
    total_rows = local_rows * shard_count
    repeats = HEADS // KV_HEADS
    local_groups = key_heads.shape[1] // HEAD_DIM
    scaling = HEAD_DIM ** (-0.5)
    positions = token_positions(span_place, total_rows, 2 * shard_count)
    samples = sample_ids(positions, sample_lengths)
    my_positions = lax.dynamic_slice_in_dim(positions, shard_index * local_rows, local_rows)
    my_samples = lax.dynamic_slice_in_dim(samples, shard_index * local_rows, local_rows)
    gathered = (
        lax.all_gather(key_heads, "dc", axis=0, tiled=True),
        lax.all_gather(value_heads, "dc", axis=0, tiled=True),
    )
    grad_full = lax.all_gather(grad_out, "tp", axis=1, tiled=True)
    head_grads = lax.dot_general(
        grad_full, out_weight, (((1,), (1,)), ((), ())), preferred_element_type=jnp.float32
    ).astype(jnp.bfloat16)
    per_block = max(1, 512 // local_rows)
    while shard_count % per_block:
        per_block -= 1
    block_rows = per_block * local_rows
    block_count = shard_count // per_block
    key_blocks = gathered[0].reshape(block_count, block_rows, local_groups, HEAD_DIM)
    value_blocks = gathered[1].reshape(block_count, block_rows, local_groups, HEAD_DIM)
    pos_blocks = positions.reshape(block_count, block_rows)
    sample_blocks = samples.reshape(block_count, block_rows)
    blocks = (key_blocks, value_blocks, pos_blocks, sample_blocks)
    query_four = query_heads.reshape(local_rows, local_groups, repeats, HEAD_DIM)
    grad_four = head_grads.reshape(local_rows, local_groups, repeats, HEAD_DIM)

    def stats_step(carry, block):
        running_top, running_total = carry
        key_block, value_block, key_pos, key_sample = block
        scores, allowed = block_scores(
            query_four, key_block, my_positions, my_samples, key_pos, key_sample, scaling
        )
        new_top = jnp.maximum(running_top, jnp.max(scores, axis=-1))
        expo = jnp.where(allowed[None, None], jnp.exp(scores - new_top[..., None]), 0.0)
        new_total = running_total * jnp.exp(running_top - new_top) + jnp.sum(expo, axis=-1)
        return ((new_top, new_total), None)

    stat_shape = (local_groups, repeats, local_rows)
    (highest, totals), unused = lax.scan(
        stats_step,
        (jnp.full(stat_shape, negative_fill, jnp.float32), jnp.zeros(stat_shape, jnp.float32)),
        blocks,
    )

    def block_probs(block):
        key_block, value_block, key_pos, key_sample = block
        scores, allowed = block_scores(
            query_four, key_block, my_positions, my_samples, key_pos, key_sample, scaling
        )
        expo = jnp.where(allowed[None, None], jnp.exp(scores - highest[..., None]), 0.0)
        return expo / totals[..., None]

    def output_step(running, block):
        weights = block_probs(block).astype(jnp.bfloat16)
        return (
            running
            + jnp.einsum("grtn,ngd->tgrd", weights, block[1], preferred_element_type=jnp.float32),
            None,
        )

    attended_sum, unused = lax.scan(
        output_step, jnp.zeros((local_rows, local_groups, repeats, HEAD_DIM), jnp.float32), blocks
    )
    attended = attended_sum.astype(jnp.bfloat16)
    attended_flat = attended.reshape(local_rows, local_groups * repeats * HEAD_DIM)
    partial_out = jnp.dot(attended_flat, out_weight, preferred_element_type=jnp.float32)
    layer_out = lax.psum_scatter(
        partial_out.astype(jnp.bfloat16), "tp", scatter_dimension=1, tiled=True
    )
    delta = jnp.sum(
        grad_four.astype(jnp.float32) * attended.astype(jnp.float32), axis=-1
    ).transpose(1, 2, 0)

    def grad_step(running, block):
        probs = block_probs(block)
        weights = probs.astype(jnp.bfloat16)
        key_block, value_block = (block[0], block[1])
        dprob = jnp.einsum(
            "tgrd,ngd->grtn", grad_four, value_block, preferred_element_type=jnp.float32
        )
        dscore = (probs * (dprob - delta[..., None])).astype(jnp.bfloat16)
        running = (
            running
            + jnp.einsum("grtn,ngd->tgrd", dscore, key_block, preferred_element_type=jnp.float32)
            * scaling
        )
        key_part = (
            jnp.einsum("grtn,tgrd->ngd", dscore, query_four, preferred_element_type=jnp.float32)
            * scaling
        )
        value_part = jnp.einsum(
            "grtn,tgrd->ngd", weights, grad_four, preferred_element_type=jnp.float32
        )
        return (running, (key_part, value_part))

    query_sum, (key_parts, value_parts) = lax.scan(
        grad_step, jnp.zeros((local_rows, local_groups, repeats, HEAD_DIM), jnp.float32), blocks
    )
    grad_queries = query_sum.reshape(local_rows, -1).astype(jnp.bfloat16)
    group_cols = local_groups * HEAD_DIM
    key_value_all = jnp.concatenate(
        (key_parts.reshape(total_rows, group_cols), value_parts.reshape(total_rows, group_cols)),
        axis=1,
    )
    key_value_mine = lax.psum_scatter(
        key_value_all.astype(jnp.bfloat16), "dc", scatter_dimension=0, tiled=True
    ).astype(jnp.float32)
    grad_keys = key_value_mine[:, :group_cols].astype(jnp.bfloat16)
    grad_values = key_value_mine[:, group_cols:].astype(jnp.bfloat16)
    weight_term = lax.dot_general(
        attended_flat, grad_full, (((0,), (0,)), ((), ())), preferred_element_type=jnp.float32
    )
    grad_weight = lax.psum_scatter(
        weight_term.astype(jnp.bfloat16), "dc", scatter_dimension=1, tiled=True
    )
    return (layer_out, grad_queries, grad_keys, grad_values, grad_weight)


def solution(mesh):
    in_specs = (P("dc", "tp"), P("dc", "tp"), P("dc", "tp"), P("tp", None), P("dc", "tp"), P(), P())
    out_specs = (P("dc", "tp"), P("dc", "tp"), P("dc", "tp"), P("dc", "tp"), P("tp", "dc"))
    return jax.shard_map(
        on_device, mesh=mesh, in_specs=in_specs, out_specs=out_specs, check_vma=False
    )
```

profile of v0, /device:TPU:0, one launch (start us, length us, event | category | flops | bytes accessed | tf_op | source)
XLA Modules:
  0.0 529.5 jit_solution(11939981596907332704)
XLA Ops:
  11.3 27.7 %all_gather.10 = bf16[3584,128]{1,0:T(8,128)(2,1)S(1)} all-gather(bf16[224,128]{1,0:T(8,128)(2,1)} %param.14), channel_id=1, replica_groups=mesh['dc'=16,'tp'=8] {'dc'}, dimensions={0}, use_global_device_ids=true | all-gather | bytes 974848 | tf_op jit(solution)/shard_map/all_gather | solution.py:54
  39.0 16.1 %while.39 = (s32[]{:T(128)}, f32[1,8,224]{2,1,0:T(8,128)S(1)}, f32[1,8,224]{2,1,0:T(8,128)S(1)}, s32[8,448]{1,0:T(8,128)S(1)}, s32[224]{0:T(256)S(1)}, /*index=5...) while((s32[]{:T(128)}, f32[1,8,224]{2,1,0:T(8,128)S(1)}, ...), condition=%wide.region_6.7_spmd.clone, body=%wide.region_3.6_spmd.clone.sunk | while | flops 212253440 | bytes 7417224 | solution.py:86
  55.1 28.5 %all_gather.9 = bf16[3584,128]{1,0:T(8,128)(2,1)S(1)} all-gather(bf16[224,128]{1,0:T(8,128)(2,1)S(1)} %copy-done.1), channel_id=1, replica_groups=mesh['dc'=16,'tp'=8] {'dc'}, dimensions={0}, use_global_device_ids=true | all-gather | bytes 974848 | tf_op jit(solution)/shard_map/all_gather | solution.py:55
  83.6 31.8 %while.40 = (s32[]{:T(128)}, f32[224,1,8,128]{3,0,2,1:T(8,128)}, bf16[8,448,1,128]{3,1,2,0:T(8,128)(2,1)S(1)}, s32[8,448]{1,0:T(8,128)S(1)}, s32[224]{0:T(256)S(...) while((s32[]{:T(128)}, f32[224,1,8,128]{3,0,2,1:T(8,128)}, ...), condition=%wide.region_8.9_spmd.clone, body=%wide.region_7.8_spmd.clone.sunk | while | flops 416618496 | bytes 2768786 | solution.py:108
  83.8 2.7 fusion.133
  86.7 3.9 fusion.133
  90.9 3.9 fusion.133
  95.0 3.9 fusion.133
  99.1 3.9 fusion.133
  103.2 3.9 fusion.133
  107.4 3.9 fusion.133
  111.5 3.9 fusion.133
  115.4 13.1 %fusion.85 = bf16[28,8,8,128]{3,1,2,0:T(8,128)(2,1)} fusion(bf16[224,8192]{1,0:T(8,128)(2,1)} %all-gather.2.cloned.1.call-done, bf16[1024,8192]{1,0:T(8,128)(2,1)} %param.16), kind=kOutput, calls=%fused_computation.80 | convolution fusion | flops 3758325760 | bytes 20905984 | tf_op jit(solution)/shard_map/dot_general | solution.py:58
  129.7 1.5 multiply_reduce_fusion
  131.2 54.9 %while.41 = (s32[]{:T(128)}, f32[224,1,8,128]{3,0,2,1:T(8,128)S(1)}, bf16[8,448,1,128]{3,1,2,0:T(8,128)(2,1)}, bf16[8,448,1,128]{3,1,2,0:T(8,128)(2,1)}, bf16[8,...) while((s32[]{:T(128)}, ...), condition=%wide.region_12.13_spmd.clone, body=%wide.region_11.12_spmd.clone.sunk | while | flops 1035876352 | bytes 19404232 | solution.py:143
  132.7 1.3 fusion.148
  134.0 1.6 fusion.145
  136.8 1.3 fusion.147
  138.3 1.3 fusion.144
  139.6 1.3 fusion.148
  140.9 1.6 fusion.145
  143.7 1.3 fusion.147
  146.4 1.3 fusion.148
  147.7 1.6 fusion.145
  150.5 1.3 fusion.147
  153.3 1.3 fusion.148
  154.6 1.6 fusion.145
  157.4 1.3 fusion.147
  158.9 1.3 fusion.144
  160.2 1.3 fusion.148
  161.5 1.6 fusion.145
  164.3 1.3 fusion.147
  167.1 1.3 fusion.148
  168.4 1.6 fusion.145
  171.1 1.3 fusion.147
  173.9 1.3 fusion.148
  175.2 1.6 fusion.145
  178.0 1.3 fusion.147
  180.8 1.3 fusion.148
  182.1 1.6 fusion.145
  184.9 1.3 fusion.147
  186.2 3.0 pad_maximum_fusion
  189.6 12.0 %convolution_convert_fusion.1 = bf16[224,8192]{1,0:T(8,128)(2,1)} fusion(bf16[1024,8192]{1,0:T(8,128)(2,1)} %param.16, bf16[28,8,8,128]{3,2,1,0:T(8,128)(2,1)S(1)} %bitcast.311), kind=kOutput, calls=%fused_computation.77 | convolution fusion | flops 3759931392 | bytes 20905984 | tf_op jit(solution)/shard_map/dot_general | solution.py:113
  201.6 10.2 %convolution_convert_fusion = bf16[1024,8192]{1,0:T(8,128)(2,1)} fusion(bf16[224,8192]{1,0:T(8,128)(2,1)} %all-gather.2.cloned.1.call-done, bf16[28,8,8,128]{3,2,1,0:T(8,128)(2,1)S(1)} %bitcast.312), kind=kOutput, calls=%fused_computation.76 | convolution fusion | flops 3766484992 | bytes 20905984 | tf_op jit(solution)/shard_map/dot_general | solution.py:157
  213.0 39.6 %reduce-scatter.6.cloned.1.call-done = bf16[224,256]{1,0:T(8,128)(2,1)} async-done(((bf16[3584,256]{1,0:T(8,128)(2,1)}), bf16[224,256]{1,0:T(8,128)(2,1)}) %reduce-scatter.6.cloned.1.call-update) | async-done | bytes 114704 | tf_op jit(solution)/shard_map/reduce_scatter | solution.py:152
  252.6 1.5 fusion.102
  254.1 84.5 %reduce-scatter.4.cloned.1.call-done = bf16[224,1024]{1,0:T(8,128)(2,1)} async-done(((bf16[224,8192]{1,0:T(8,128)(2,1)}), bf16[224,1024]{1,0:T(8,128)(2,1)}) %reduce-scatter.4.cloned.1.call-update) | async-done | bytes 458768 | tf_op jit(solution)/shard_map/reduce_scatter | solution.py:114
  338.6 184.4 %reduce-scatter.8.cloned.1.call-done = bf16[1024,512]{1,0:T(8,128)(2,1)} async-done(((bf16[1024,8192]{1,0:T(8,128)(2,1)}), bf16[1024,512]{1,0:T(8,128)(2,1)}) %reduce-scatter.8.cloned.1.call-update) | async-done | bytes 1048592 | tf_op jit(solution)/shard_map/reduce_scatter | solution.py:160
  (139 shorter events, 42.6 us)
Async XLA Ops:
  7.2 108.2 %all-gather.2.cloned.1.call-start = ((), (), s32[]{:S(2)}) async-start(), calls=%async_computation.4 | async-start | bytes 4128768 | tf_op jit(solution)/shard_map/all_gather | solution.py:57
  7.9 244.7 %reduce-scatter.6.cloned.1.call-start = ((), (), s32[]{:S(2)}) async-start(), calls=%async_computation.5 | async-start | bytes 1949696 | tf_op jit(solution)/shard_map/reduce_scatter | solution.py:152
  39.0 16.1 %copy-start.1 = (bf16[224,128]{1,0:T(8,128)(2,1)S(1)}, bf16[224,128]{1,0:T(8,128)(2,1)}, u32[]{:S(2)}) copy-start(bf16[224,128]{1,0:T(8,128)(2,1)} %param.15) | copy-start | bytes 172036
  115.4 13.1 %copy-start = (bf16[8,448,1,128]{3,1,2,0:T(8,128)(2,1)}, bf16[8,448,1,128]{3,1,2,0:T(8,128)(2,1)S(1)}, u32[]{:S(2)}) copy-start(bf16[8,448,1,128]{3,1,2,0:T(8,128)(2,1)S(1)} %get-tuple-element.845) | copy-start | bytes 2752516
  189.2 149.5 %reduce-scatter.4.cloned.1.call-start = ((), (), s32[]{:S(2)}) async-start(), calls=%async_computation.3 | async-start | bytes 4128768 | tf_op jit(solution)/shard_map/reduce_scatter | solution.py:114
  201.6 321.4 %reduce-scatter.8.cloned.1.call-start = ((), (), s32[]{:S(2)}) async-start(), calls=%async_computation.6 | async-start | bytes 17825792 | tf_op jit(solution)/shard_map/reduce_scatter | solution.py:160
Sparse Core Ops, SparseCore 0:
  10.3 79.1 all-gather.1
  189.3 63.3 reduce-scatter.5
  257.6 80.9 reduce-scatter.3
  341.6 181.3 reduce-scatter.7
where the time goes:
time: 530 us
  waiting for transfers between devices  309 us (58%)
  matrix products  125 us (24%)
  blocking collectives  56.2 us (11%)
  other arithmetic  18.6 us (4%)
  between operations  13.9 us (3%)
  local copies, waits for them, and re-layouts  5.55 us (1%)
    reduce_scatter x1, waiting for transfers between devices, on_device(): lax.psum_scatter(weight_term.astype(jnp.bfloat16), 'dc', scatter_dimensio...  184 us
    reduce_scatter x1, waiting for transfers between devices, on_device(): lax.psum_scatter(partial_out.astype(jnp.bfloat16), 'tp', scatter_dimensio...  84.5 us
    reduce_scatter x1, waiting for transfers between devices, on_device(): lax.psum_scatter(key_value_all.astype(jnp.bfloat16), 'dc', scatter_dimens...  39.6 us
    dot_general x8, matrix products, output_step(): jnp.einsum('grtn,ngd->tgrd', weights, block[1], preferred_element_type=jn...  30.2 us
    all_gather x1, blocking collectives, on_device(): lax.all_gather(value_heads, 'dc', axis=0, tiled=True)  28.5 us
    all_gather x1, blocking collectives, on_device(): lax.all_gather(key_heads, 'dc', axis=0, tiled=True)  27.7 us
    dot_general x16, matrix products, block_scores(): jnp.einsum('tgrd,ngd->grtn', query_four, key_block, preferred_element_typ...  16.3 us
    dot_general x1, matrix products, on_device(): lax.dot_general(grad_full, out_weight, (((1,), (1,)), ((), ())), preferre...  13.1 us
  transfers between devices with their start and end apart: 4, of which 3 were waited for; matrix products, arithmetic and copies ran while one was open for 14% of the time, Pallas kernels for 0%

commit v1 on v0

v1 whole, which is shorter than its diff:
```python
import functools

import jax
import jax.numpy as jnp
from jax import lax
from jax.experimental import pallas as pl
from jax.experimental.pallas import tpu as pltpu
from jax.sharding import PartitionSpec as P

HEAD_DIM = 128
ROWS = 224
SPAN = 112
GROUP = 8
ZK = 896
COLS = 1024
HALF = 112
SCALE = HEAD_DIM**-0.5
SCALE2 = SCALE * 1.4426950408889634
FILL = -1e30
MESH = pl.DeviceIdType.MESH
F32 = jnp.float32
BF16 = jnp.bfloat16


def dot_nn(a, b):
    return lax.dot_general(a, b, (((1,), (0,)), ((), ())), preferred_element_type=F32)


def dot_nt(a, b):
    return lax.dot_general(a, b, (((1,), (1,)), ((), ())), preferred_element_type=F32)


def dot_tn(a, b):
    return lax.dot_general(a, b, (((0,), (0,)), ((), ())), preferred_element_type=F32)


class Here:
    def __init__(self):
        d = lax.axis_index("dc")
        t = lax.axis_index("tp")
        self.d, self.t = d, t
        self.c = lax.rem(d, 2)
        self.x = lax.rem(lax.div(d, 2), 2)
        self.z = lax.div(d, 4)
        self.h = lax.rem(t, 2)
        self.y = lax.div(t, 2)

    def by_dc(self, z, x):
        return ((z * 2 + x) * 2 + self.c, self.t)

    def by_tp(self, y, h):
        return (self.d, y * 2 + h)

    def sibling(self):
        return ((self.z * 2 + self.x) * 2 + (1 - self.c), self.t)


def around(a):
    return lax.rem(a + 1, 4), lax.rem(a + 3, 4), lax.rem(a + 2, 4)


def meet(devices):
    barrier = pltpu.get_barrier_semaphore()
    for device in devices:
        pl.semaphore_signal(barrier, inc=1, device_id=device, device_id_type=MESH)
    pl.semaphore_wait(barrier, len(devices))


class Gather:
    def __init__(self, view, a, b, dev, ssem, rsem):
        up, dn, far = around(a)
        o = 1 - b
        self.view, self.ssem, self.rsem = view, ssem, rsem
        self.out = [
            (a, b, None, dev(a, o)),
            (a, b, None, dev(up, b)),
            (a, b, None, dev(dn, b)),
            (a, o, None, dev(up, b)),
            (a, o, None, dev(dn, b)),
            (dn, b, 0, dev(up, b)),
            (up, b, 1, dev(dn, b)),
            (dn, o, 0, dev(up, b)),
            (up, o, 1, dev(dn, b)),
        ]
        self.into = [
            (a, o, None),
            (dn, b, None),
            (up, b, None),
            (dn, o, None),
            (up, o, None),
            (far, b, 0),
            (far, b, 1),
            (far, o, 0),
            (far, o, 1),
        ]

    def sent(self, i):
        a, b, half, device = self.out[i]
        ref = self.view(a, b, half)
        return pltpu.make_async_remote_copy(
            ref, ref, self.ssem.at[i], self.rsem.at[i], device_id=device, device_id_type=MESH
        )

    def got(self, i):
        a, b, half = self.into[i]
        ref = self.view(a, b, half)
        pltpu.make_async_remote_copy(
            ref, ref, self.ssem.at[i], self.rsem.at[i], device_id=self.out[i][3], device_id_type=MESH
        ).wait_recv()

    def start(self):
        for i in (1, 2, 0):
            self.sent(i).start()

    def pair(self):
        self.got(0)
        self.sent(3).start()
        self.sent(4).start()

    def near(self):
        self.got(1)
        self.sent(5).start()
        self.got(2)
        self.sent(6).start()

    def near_pair(self):
        self.got(3)
        self.sent(7).start()
        self.got(4)
        self.sent(8).start()

    def far(self):
        self.got(5)
        self.got(6)

    def far_pair(self):
        self.got(7)
        self.got(8)

    def drain(self):
        for i in range(9):
            self.sent(i).wait_send()


class Sibling:
    def __init__(self, view, here, ssem, rsem):
        up, dn, far = around(here.z)
        x, o = here.x, 1 - here.x
        self.here, self.view, self.ssem, self.rsem = here, view, ssem, rsem
        self.blocks = [
            (here.z, x), (here.z, o), (dn, x), (up, x), (dn, o), (up, o), (far, x), (far, o),
        ]

    def sent(self, i, core):
        z, x = self.blocks[i]
        ref = self.view(z, x, core)
        return pltpu.make_async_remote_copy(
            ref, ref, self.ssem.at[i], self.rsem.at[i],
            device_id=self.here.sibling(), device_id_type=MESH,
        )

    def start(self, *order):
        for i in order:
            self.sent(i, self.here.c).start()

    def got(self, *order):
        for i in order:
            self.sent(i, 1 - self.here.c).wait_recv()

    def drain(self):
        for i in range(8):
            self.sent(i, self.here.c).wait_send()


class Reduce:
    def __init__(self, emit, a, b, dev, sbuf, rbuf, ssem, rsem):
        up, dn, far = around(a)
        self.emit, self.b, self.sbuf, self.rbuf, self.ssem, self.rsem = emit, b, sbuf, rbuf, ssem, rsem
        u, d, p = dev(up, b), dev(dn, b), dev(a, 1 - b)
        self.devices = [u, d, u, d, u, d, p]

    def copy(self, i):
        return pltpu.make_async_remote_copy(
            self.sbuf.at[i], self.rbuf.at[i], self.ssem.at[i], self.rsem.at[i],
            device_id=self.devices[i], device_id_type=MESH,
        )

    def send(self, i, which, b, adds=()):
        self.emit(self.sbuf.at[i], which, b, [self.rbuf.at[j] for j in adds])
        self.copy(i).start()

    def far(self):
        self.send(0, "far", 0)
        self.send(1, "far", 1)

    def near(self):
        self.send(2, "up", 1)
        self.send(3, "dn", 0)

    def comb(self):
        self.copy(0).wait_recv()
        self.send(4, "up", 0, [0])
        self.copy(1).wait_recv()
        self.send(5, "dn", 1, [1])

    def pair(self):
        for i in (2, 3, 4, 5):
            self.copy(i).wait_recv()
        o = 1 - self.b
        self.send(6, "own", o, [4 + o, 3 - o])

    def final(self, out):
        self.copy(6).wait_recv()
        b = self.b
        self.emit(out, "own", b, [self.rbuf.at[j] for j in (4 + b, 3 - b, 6)])

    def drain(self):
        for i in range(7):
            self.copy(i).wait_send()


def write_bias(bias, place_ref, length_ref, here):
    row = lax.broadcasted_iota(jnp.int32, (ROWS, 1), 0)
    first, second = place_ref[2 * here.d], place_ref[2 * here.d + 1]
    pos = row + jnp.where(row < SPAN, first * SPAN, second * SPAN - SPAN)
    low = jnp.zeros((ROWS, 1), jnp.int32)
    bound = length_ref[0]
    for i in range(1, 4):
        low = jnp.where(pos >= bound, bound, low)
        bound = bound + length_ref[i]

    def fill(z, carry):
        lane = lax.broadcasted_iota(jnp.int32, (1, ZK), 1)
        key = jnp.zeros((1, ZK), jnp.int32)
        for i in range(8):
            begin = place_ref[8 * z + i] * SPAN - i * SPAN
            key = jnp.where(lane >= i * SPAN, lane + begin, key)
        bias[z] = jnp.where((key >= low) & (key <= pos), 0.0, FILL)
        return carry

    lax.fori_loop(0, 4, fill, 0)


def split_heads(dst, src):
    for head in range(GROUP):
        dst[head] = src[:, head * HEAD_DIM : (head + 1) * HEAD_DIM]


def keys_of(kv, which, z):
    return kv[which, pl.ds(4 * z, 4)].reshape(ZK, HEAD_DIM)


def forward_kernel(
    q_ref, k_ref, v_ref, w_ref, g_ref, place_ref, length_ref,
    att_ref, hg_ref, lse_ref, kv_out,
    kv, gbuf, wbuf, q_s, bias, top, total, oacc, hacc,
    wsem, kv_s, kv_r, sib_s, sib_r, g_s, g_r, out_sem,
):
    here = Here()

    def load_w(j):
        return pltpu.make_async_copy(w_ref.at[:, pl.ds(j * COLS, COLS)], wbuf.at[j], wsem.at[j])

    def kv_view(z, x, core, half=None):
        slot = (z * 2 + x) * 2 + core
        if half is None:
            return kv.at[:, slot]
        return kv.at[:, slot, pl.ds(half * HALF, HALF)]

    def g_view(y, h, half):
        if half is None:
            return gbuf.at[y * 2 + h]
        return gbuf.at[y * 2 + h, pl.ds(half * HALF, HALF)]

    kv[0, here.d] = k_ref[...]
    kv[1, here.d] = v_ref[...]
    gbuf[here.t] = g_ref[...]
    kvg = Gather(lambda z, x, half: kv_view(z, x, here.c, half), here.z, here.x, here.by_dc, kv_s, kv_r)
    sib = Sibling(kv_view, here, sib_s, sib_r)
    gg = Gather(g_view, here.y, here.h, here.by_tp, g_s, g_r)
    zu, zd, _ = around(here.z)
    yu, yd, _ = around(here.y)
    meet([
        here.by_dc(zu, here.x), here.by_dc(zd, here.x), here.by_dc(here.z, 1 - here.x), here.sibling(),
        here.by_tp(yu, here.h), here.by_tp(yd, here.h), here.by_tp(here.y, 1 - here.h),
    ])
    kvg.start()
    sib.start(0)
    gg.start()
    for j in range(8):
        load_w(j).start()
    split_heads(q_s, q_ref)
    write_bias(bias, place_ref, length_ref, here)
    top[...] = jnp.full(top.shape, FILL, F32)
    total[...] = jnp.zeros(total.shape, F32)
    oacc[...] = jnp.zeros(oacc.shape, F32)
    hacc[...] = jnp.zeros(hacc.shape, F32)
    kvg.pair()
    sib.start(1)
    kvg.near()
    sib.start(2, 3)
    kvg.near_pair()
    sib.start(4, 5)
    kvg.far()
    sib.start(6)
    kvg.far_pair()
    sib.start(7)
    sib.got(*range(8))
    gg.near()
    gg.pair()
    copies = pltpu.make_async_copy(kv, kv_out, out_sem)
    copies.start()

    def scores(z, g):
        q = q_s[pl.ds(2 * g, 2)].reshape(2 * ROWS, HEAD_DIM)
        s = dot_nt(q, keys_of(kv, 0, z)) * SCALE2
        s = s.reshape(2, ROWS, ZK) + bias[z][None]
        return s.reshape(2 * ROWS, ZK)

    def maxima(i, carry):
        z, g = lax.div(i, 4), lax.rem(i, 4)
        s = scores(z, g)
        high = top[g]
        for j in range(ZK // 128):
            high = jnp.maximum(high, s[:, j * 128 : (j + 1) * 128])
        top[g] = high
        return carry

    def outputs(i, carry):
        z, g = lax.div(i, 4), lax.rem(i, 4)
        p = jnp.exp2(scores(z, g) - top[g][:, :1])
        part = total[g]
        for j in range(ZK // 128):
            part = part + p[:, j * 128 : (j + 1) * 128]
        total[g] = part
        oacc[g] += dot_nn(p.astype(BF16), keys_of(kv, 1, z))
        return carry

    lax.fori_loop(0, 16, maxima, 0)

    def spread(g, carry):
        top[g] = jnp.broadcast_to(jnp.max(top[g], axis=1, keepdims=True), (2 * ROWS, 128))
        return carry

    lax.fori_loop(0, 4, spread, 0)
    lax.fori_loop(0, 16, outputs, 0)
    for g in range(4):
        whole = jnp.broadcast_to(jnp.sum(total[g], axis=1, keepdims=True), (2 * ROWS, 128))
        lse_ref[g] = top[g] + jnp.log2(whole)
        o = (oacc[g] / whole).astype(BF16)
        for j in range(2):
            head = 2 * g + j
            att_ref[:, head * HEAD_DIM : (head + 1) * HEAD_DIM] = o[j * ROWS : (j + 1) * ROWS]

    gg.near_pair()

    def head_grads(y, h):
        slot = y * 2 + h

        def tile(n, carry):
            cols = pl.ds(pl.multiple_of(n * 256, 256), 256)
            hacc[:, cols] += dot_nt(gbuf[slot], wbuf[slot, cols, :])
            return carry

        lax.fori_loop(0, 4, tile, 0)

    for j in range(8):
        load_w(j).wait()
    far = around(here.y)[2]
    o = 1 - here.h
    for y, h in ((here.y, here.h), (here.y, o), (yd, here.h), (yu, here.h), (yd, o), (yu, o)):
        head_grads(y, h)
    gg.far()
    head_grads(far, here.h)
    gg.far_pair()
    head_grads(far, o)
    hg_ref[...] = hacc[...].astype(BF16)
    copies.wait()
    kvg.drain()
    sib.drain()
    gg.drain()


def backward_kernel(
    q_ref, kv, att_ref, hg_ref, lse_ref, same_ref, cross_ref, w_ref, place_ref, length_ref,
    out_ref, dq_ref, dk_ref, dv_ref, gw_ref,
    attall, gcol, wbuf, q_s, do_s, qt_s, dot_s, delta, bias, dqacc, kt, vt, keep, sib_out, sib_in,
    c_out, c_in, d_out, d_in, d_final, gacc,
    wsem, att_s, att_r, sib_s, sib_r, col_s, col_r, c_s, c_r, x_s, x_r, d_s, d_r,
):
    here = Here()

    def load_w(j):
        return pltpu.make_async_copy(w_ref.at[:, pl.ds(j * COLS, COLS)], wbuf.at[j], wsem.at[j])

    for j in range(8):
        load_w(j).start()

    def att_view(z, x, core, half=None):
        slot = (z * 2 + x) * 2 + core
        if half is None:
            return attall.at[slot]
        return attall.at[slot, pl.ds(half * HALF, HALF)]

    def col_view(y, h, half):
        if half is None:
            return gcol.at[y * 2 + h]
        return gcol.at[y * 2 + h, half]

    attall[here.d] = att_ref[...]
    gcol[here.t, here.c] = same_ref[...]
    gcol[here.t, 1 - here.c] = cross_ref[...]
    ag = Gather(lambda z, x, half: att_view(z, x, here.c, half), here.z, here.x, here.by_dc, att_s, att_r)
    sib = Sibling(att_view, here, sib_s, sib_r)
    cg = Gather(col_view, here.y, here.h, here.by_tp, col_s, col_r)
    zu, zd, zf = around(here.z)
    yu, yd, yf = around(here.y)
    meet([
        here.by_dc(zu, here.x), here.by_dc(zd, here.x), here.by_dc(here.z, 1 - here.x), here.sibling(),
        here.by_tp(yu, here.h), here.by_tp(yd, here.h), here.by_tp(here.y, 1 - here.h),
    ])
    ag.start()
    sib.start(0)

    def out_part(dst, which, h, adds):
        slot = {"far": yf, "up": yu, "dn": yd, "own": here.y}[which] * 2 + h

        def tile(n, carry):
            cols = pl.ds(pl.multiple_of(n * 256, 256), 256)
            acc = dot_nn(att_ref[...], wbuf[slot, :, cols])
            for add in adds:
                acc = acc + add[:, cols].astype(F32)
            dst[:, cols] = acc.astype(BF16)
            return carry

        lax.fori_loop(0, 4, tile, 0)

    c_red = Reduce(out_part, here.y, here.h, here.by_tp, c_out, c_in, c_s, c_r)

    def kv_part(dst, which, x, adds):
        r = {"far": 0, "dn": 1, "up": 2, "own": 3}[which]
        acc = keep[r, x] + sib_in[r, x].astype(F32)
        for add in adds:
            acc = acc + add[...].astype(F32)
        dst[...] = acc.astype(BF16)

    d_red = Reduce(kv_part, here.z, here.x, here.by_dc, d_out, d_in, d_s, d_r)

    def sib_sum(r):
        return pltpu.make_async_remote_copy(
            sib_out.at[r], sib_in.at[r], x_s.at[r], x_r.at[r],
            device_id=here.sibling(), device_id_type=MESH,
        )

    for j in range(8):
        load_w(j).wait()
    c_red.far()
    c_red.near()
    cg.start()

    split_heads(q_s, q_ref)
    split_heads(do_s, hg_ref)
    write_bias(bias, place_ref, length_ref, here)
    dqacc[...] = jnp.zeros(dqacc.shape, F32)
    for g in range(4):
        for j in range(2):
            head = 2 * g + j
            a = att_ref[:, head * HEAD_DIM : (head + 1) * HEAD_DIM].astype(F32)
            d = do_s[head].astype(F32)
            delta[g, pl.ds(j * ROWS, ROWS)] = jnp.broadcast_to(
                jnp.sum(a * d, axis=1, keepdims=True), (ROWS, 128)
            )
        qt_s[g] = q_s[pl.ds(2 * g, 2)].reshape(2 * ROWS, HEAD_DIM).T
        dot_s[g] = do_s[pl.ds(2 * g, 2)].reshape(2 * ROWS, HEAD_DIM).T

    def plane(r, z):
        kt[...] = jnp.zeros(kt.shape, F32)
        vt[...] = jnp.zeros(vt.shape, F32)

        def step(g, carry):
            k, v = keys_of(kv, 0, z), keys_of(kv, 1, z)
            q = q_s[pl.ds(2 * g, 2)].reshape(2 * ROWS, HEAD_DIM)
            do = do_s[pl.ds(2 * g, 2)].reshape(2 * ROWS, HEAD_DIM)
            s = dot_nt(q, k) * SCALE2
            s = (s.reshape(2, ROWS, ZK) + bias[z][None]).reshape(2 * ROWS, ZK)
            p = jnp.exp2(s - lse_ref[g][:, :1])
            ds = (p * (dot_nt(do, v) - delta[g][:, :1])).astype(BF16)
            dqacc[g] += dot_nn(ds, k)
            kt[...] += dot_nn(qt_s[g], ds)
            vt[...] += dot_nn(dot_s[g], p.astype(BF16))
            return carry

        lax.fori_loop(0, 4, step, 0)
        dk = (kt[...] * SCALE).T.reshape(4, ROWS, HEAD_DIM)
        dv = vt[...].T.reshape(4, ROWS, HEAD_DIM)
        for x in range(2):
            mine = here.c == 0
            for which, value in ((0, dk), (1, dv)):
                even, odd = value[2 * x], value[2 * x + 1]
                keep[r, x, which] = jnp.where(mine, even, odd)
                sib_out[r, x, which] = jnp.where(mine, odd, even).astype(BF16)
        sib_sum(r).start()

    plane(0, zf)
    ag.pair()
    sib.start(1)
    ag.near()
    sib.start(2, 3)
    c_red.comb()
    plane(1, zd)
    sib_sum(0).wait_recv()
    d_red.far()
    ag.near_pair()
    sib.start(4, 5)
    cg.pair()
    plane(2, zu)
    sib_sum(1).wait_recv()
    sib_sum(2).wait_recv()
    d_red.near()
    cg.near()
    c_red.pair()
    plane(3, here.z)
    d_red.comb()
    ag.far()
    sib.start(6)
    ag.far_pair()
    sib.start(7)
    cg.near_pair()
    for g in range(4):
        value = (dqacc[g] * SCALE).astype(BF16)
        for j in range(2):
            head = 2 * g + j
            dq_ref[:, head * HEAD_DIM : (head + 1) * HEAD_DIM] = value[j * ROWS : (j + 1) * ROWS]
    sib_sum(3).wait_recv()
    d_red.pair()
    sib.got(*range(8))
    gacc[...] = jnp.zeros(gacc.shape, F32)

    def weight_part(y, h):
        chip = lax.rem(y - here.z + 4, 4) * 2 + h
        right = gcol[y * 2 + h].reshape(2 * ROWS, COLS // 2)

        def tile(n, carry):
            cols = pl.ds(pl.multiple_of(n * 256, 256), 256)
            left = attall[pl.ds(2 * chip, 2), :, cols].reshape(2 * ROWS, 256)
            gacc[cols, :] += dot_tn(left, right)
            return carry

        lax.fori_loop(0, 4, tile, 0)

    o = 1 - here.h
    for y, h in ((here.y, here.h), (here.y, o), (yd, here.h), (yu, here.h), (yd, o), (yu, o)):
        weight_part(y, h)
    d_red.final(d_final)
    dk_ref[...] = d_final[0]
    dv_ref[...] = d_final[1]
    c_red.final(out_ref)
    cg.far()
    weight_part(yf, here.h)
    cg.far_pair()
    weight_part(yf, o)
    gw_ref[...] = gacc[...].astype(BF16)
    ag.drain()
    sib.drain()
    cg.drain()
    c_red.drain()
    d_red.drain()
    for r in range(4):
        sib_sum(r).wait_send()


def vmem():
    return pl.BlockSpec(memory_space=pltpu.VMEM)


def smem():
    return pl.BlockSpec(memory_space=pltpu.SMEM)


def anywhere():
    return pl.BlockSpec(memory_space=pl.ANY)


def dma(n):
    return pltpu.SemaphoreType.DMA((n,))


def forward(q, k, v, w, g, place, length):
    shape = jax.ShapeDtypeStruct
    return pl.pallas_call(
        forward_kernel,
        out_shape=(
            shape((ROWS, COLS), BF16),
            shape((ROWS, COLS), BF16),
            shape((4, 2 * ROWS, 128), F32),
            shape((2, 16, ROWS, HEAD_DIM), BF16),
        ),
        in_specs=[vmem(), vmem(), vmem(), anywhere(), vmem(), smem(), smem()],
        out_specs=(vmem(), vmem(), vmem(), anywhere()),
        scratch_shapes=[
            pltpu.VMEM((2, 16, ROWS, HEAD_DIM), BF16),
            pltpu.VMEM((8, ROWS, COLS), BF16),
            pltpu.VMEM((8, COLS, COLS), BF16),
            pltpu.VMEM((GROUP, ROWS, HEAD_DIM), BF16),
            pltpu.VMEM((4, ROWS, ZK), F32),
            pltpu.VMEM((4, 2 * ROWS, 128), F32),
            pltpu.VMEM((4, 2 * ROWS, 128), F32),
            pltpu.VMEM((4, 2 * ROWS, 128), F32),
            pltpu.VMEM((ROWS, COLS), F32),
            dma(8), dma(9), dma(9), dma(8), dma(8), dma(9), dma(9),
            pltpu.SemaphoreType.DMA,
        ],
        compiler_params=pltpu.CompilerParams(
            collective_id=0, has_side_effects=True, vmem_limit_bytes=58 * 2**20
        ),
        cost_estimate=pl.CostEstimate(flops=9 * 10**9, bytes_accessed=24 * 10**6, transcendentals=6 * 10**6),
    )(q, k, v, w, g, place, length)


def backward(q, kv, att, hg, lse, same, cross, w, place, length):
    shape = jax.ShapeDtypeStruct
    return pl.pallas_call(
        backward_kernel,
        out_shape=(
            shape((ROWS, COLS), BF16),
            shape((ROWS, COLS), BF16),
            shape((ROWS, HEAD_DIM), BF16),
            shape((ROWS, HEAD_DIM), BF16),
            shape((COLS, COLS // 2), BF16),
        ),
        in_specs=[vmem()] * 7 + [anywhere(), smem(), smem()],
        out_specs=(vmem(),) * 5,
        scratch_shapes=[
            pltpu.VMEM((16, ROWS, COLS), BF16),
            pltpu.VMEM((8, 2, ROWS, COLS // 2), BF16),
            pltpu.VMEM((8, COLS, COLS), BF16),
            pltpu.VMEM((GROUP, ROWS, HEAD_DIM), BF16),
            pltpu.VMEM((GROUP, ROWS, HEAD_DIM), BF16),
            pltpu.VMEM((4, HEAD_DIM, 2 * ROWS), BF16),
            pltpu.VMEM((4, HEAD_DIM, 2 * ROWS), BF16),
            pltpu.VMEM((4, 2 * ROWS, 128), F32),
            pltpu.VMEM((4, ROWS, ZK), F32),
            pltpu.VMEM((4, 2 * ROWS, 128), F32),
            pltpu.VMEM((HEAD_DIM, ZK), F32),
            pltpu.VMEM((HEAD_DIM, ZK), F32),
            pltpu.VMEM((4, 2, 2, ROWS, HEAD_DIM), F32),
            pltpu.VMEM((4, 2, 2, ROWS, HEAD_DIM), BF16),
            pltpu.VMEM((4, 2, 2, ROWS, HEAD_DIM), BF16),
            pltpu.VMEM((7, ROWS, COLS), BF16),
            pltpu.VMEM((7, ROWS, COLS), BF16),
            pltpu.VMEM((7, 2, ROWS, HEAD_DIM), BF16),
            pltpu.VMEM((7, 2, ROWS, HEAD_DIM), BF16),
            pltpu.VMEM((2, ROWS, HEAD_DIM), BF16),
            pltpu.VMEM((COLS, COLS // 2), F32),
            dma(8), dma(9), dma(9), dma(8), dma(8), dma(9), dma(9), dma(7), dma(7), dma(4), dma(4),
            dma(7), dma(7),
        ],
        compiler_params=pltpu.CompilerParams(
            collective_id=1, has_side_effects=True, vmem_limit_bytes=62 * 2**20
        ),
        cost_estimate=pl.CostEstimate(flops=16 * 10**9, bytes_accessed=30 * 10**6, transcendentals=6 * 10**6),
    )(q, kv, att, hg, lse, same, cross, w, place, length)


def permutation(flip):
    pairs = []
    for d in range(16):
        z, x, c = d // 4, d // 2 % 2, d % 2
        for t in range(8):
            y, h = t // 2, t % 2
            to = ((y * 2 + h) * 2 + (c ^ flip)) * 8 + (y + z) % 4 * 2 + x
            pairs.append((d * 8 + t, to))
    return pairs


def on_device(q, k, v, w, g, place, length):
    core = lax.rem(lax.axis_index("dc"), 2)
    half = COLS // 2
    same = lax.ppermute(
        lax.dynamic_slice_in_dim(g, core * half, half, axis=1), ("dc", "tp"), permutation(0)
    )
    cross = lax.ppermute(
        lax.dynamic_slice_in_dim(g, (1 - core) * half, half, axis=1), ("dc", "tp"), permutation(1)
    )
    att, hg, lse, kv = forward(q, k, v, w, g, place, length)
    return backward(q, kv, att, hg, lse, same, cross, w, place, length)


def solution(mesh):
    in_specs = (P("dc", "tp"), P("dc", "tp"), P("dc", "tp"), P("tp", None), P("dc", "tp"), P(), P())
    out_specs = (P("dc", "tp"), P("dc", "tp"), P("dc", "tp"), P("dc", "tp"), P("tp", "dc"))
    return jax.shard_map(
        on_device, mesh=mesh, in_specs=in_specs, out_specs=out_specs, check_vma=False
    )
```

time: 530 us -> 151 us (0.28)
  waiting for transfers between devices: 309 us -> 0.01 us
  Pallas kernels: 0 us -> 137 us
  matrix products: 125 us -> 0 us
  blocking collectives: 56.2 us -> 0 us
  other arithmetic: 18.6 us -> 0 us
  between operations: 13.9 us -> 0.71 us
    reduce_scatter x3 -> x0, waiting for transfers between devices: 308 us -> none  [the longest x1 184 us: on_device(): lax.psum_scatter(weight_term.astype(jnp.bfloat16), 'dc', scatter_dimensio...]
    pallas_call x0 -> x2, Pallas kernels: none -> 137 us  [the longest x1 77.7 us: backward(): pl.pallas_call(backward_kernel, out_shape=(shape((ROWS, COLS), BF16), sha...]
    dot_general x59 -> x0, matrix products: 125 us -> none  [the longest x8 30.2 us: output_step(): jnp.einsum('grtn,ngd->tgrd', weights, block[1], preferred_element_type=jn...]
    all_gather x2 -> x0, blocking collectives: 56.2 us -> none  [the longest x1 28.5 us: on_device(): lax.all_gather(value_heads, 'dc', axis=0, tiled=True)]
    reduce_sum x11 -> x0, other arithmetic: 10 us -> none  [the longest x8 7.56 us: stats_step(): jnp.sum(expo, axis=-1)]
    unnamed x9, local copies, waits for them, and re-layouts: 3.16 us -> 9.52 us
  transfers between devices with their start and end apart: 4 -> 2, of which waited for: 3 -> 0; matrix products, arithmetic and copies ran while one was open for 14% -> 0% of each run, Pallas kernels for 0% -> 40%
where the time goes in v1:
time: 151 us; the launch traced here: 149 us
  Pallas kernels  137 us (91%)
  local copies, waits for them, and re-layouts  10.6 us (7%)
    pallas_call x1, Pallas kernels, backward(): pl.pallas_call(backward_kernel, out_shape=(shape((ROWS, COLS), BF16), sha...  77.7 us
    pallas_call x1, Pallas kernels, forward(): pl.pallas_call(forward_kernel, out_shape=(shape((ROWS, COLS), BF16), shap...  59.7 us
    unnamed x9, local copies, waits for them, and re-layouts  9.52 us
  transfers between devices with their start and end apart: 2, of which 0 were waited for; matrix products, arithmetic and copies ran while one was open for 0% of the time, Pallas kernels for 40%

profile of v1, /device:TPU:0, one launch (start us, length us, event | category | flops | bytes accessed | tf_op | source)
XLA Modules:
  0.0 149.4 jit_solution(9673243169180903631)
XLA Ops:
  0.6 1.1 constant_dynamic-slice_fusion
  1.7 0.1 collective-permute-start.1
  1.8 0.7 collective-permute-start
  2.5 59.7 %shard_map.110 = (bf16[224,1024]{1,0:T(8,128)(2,1)}, bf16[224,1024]{1,0:T(8,128)(2,1)}, f32[4,448,128]{2,1,0:T(8,128)}, bf16[2,16,224,128]{3,2,1,0:T(8,128)(2,1)}) custom-call(bf16[224,1024]{1,0:T(8,128)(2,1)} %q_ref.3, bf16[224,128]{1,0:T(8,128)(2,1)} %k_ref.1, bf16[224,128]{1,0:T(8,128)(2,1)} %v_ref.1, bf16[1024,8192]{1,0:T(8,128)(2,1)} %w_ref.3, ...), custom_call_target="tpu_custom_call" | custom-call | flops 8999999488 | bytes 24000000 | tf_op jit(solution)/shard_map/pallas_call | solution.py:590
  62.2 0.0 collective-permute-done.1.cross_ref
  62.2 0.0 copy-start
  62.2 0.0 collective-permute-done.same_ref
  62.2 0.0 copy-start.1
  62.2 0.7 copy-done
  62.9 0.1 copy-done.1
  63.0 77.7 %shard_map.111 = (bf16[224,1024]{1,0:T(8,128)(2,1)}, bf16[224,1024]{1,0:T(8,128)(2,1)}, bf16[224,128]{1,0:T(8,128)(2,1)}, bf16[224,128]{1,0:T(8,128)(2,1)}, bf16[1024,512]{1,0:T(8,128)(2,1)}) custom-call(bf16[224,1024]{1,0:T(8,128)(2,1)} %q_ref.3, bf16[2,16,224,128]{3,2,1,0:T(8,128)(2,1)} %get-tuple-element.9.kv, ...), custom_call_target="tpu_custom_call" | custom-call | flops 16000000000 | bytes 30000000 | tf_op jit(solution)/shard_map/pallas_call | solution.py:622
  140.7 1.8 %copy.17 = bf16[224,1024]{1,0:T(8,128)(2,1)} copy(bf16[224,1024]{1,0:T(8,128)(2,1)} %get-tuple-element.20) | data formatting | bytes 917504
  142.5 1.8 %copy.18 = bf16[224,1024]{1,0:T(8,128)(2,1)} copy(bf16[224,1024]{1,0:T(8,128)(2,1)} %get-tuple-element.21) | data formatting | bytes 917504
  144.3 1.4 copy.19
  145.7 1.4 copy.20
  147.2 2.3 %copy.21 = bf16[1024,512]{1,0:T(8,128)(2,1)} copy(bf16[1024,512]{1,0:T(8,128)(2,1)} %get-tuple-element.24) | data formatting | bytes 2097152
Async XLA Ops:
  1.7 60.5 %collective-permute-start.1 = (bf16[224,512]{1,0:T(8,128)(2,1)S(1)}, bf16[224,512]{1,0:T(8,128)(2,1)S(1)}, u32[]{:S(2)}, u32[]{:S(2)}) collective-permute-start(bf16[224,512]{1,0:T(8,128)(2,1)S(1)} %get-tuple-element.13), channel_id=1, source_target_pairs={{0,8},{1,24},{2,42},{3,58},{4,76},{5,92},{6,110},{7,126},{8,0},{9,... | collective-permute-start | bytes 688136 | tf_op jit(solution)/shard_map/ppermute | solution.py:682
  1.8 60.4 %collective-permute-start = (bf16[224,512]{1,0:T(8,128)(2,1)S(1)}, bf16[224,512]{1,0:T(8,128)(2,1)S(1)}, u32[]{:S(2)}, u32[]{:S(2)}) collective-permute-start(bf16[224,512]{1,0:T(8,128)(2,1)S(1)} %get-tuple-element.14), channel_id=1, source_target_pairs={{0,0},{1,16},{2,34},{3,50},{4,68},{5,84},{6,102},{7,118},{8,8},{9,... | collective-permute-start | bytes 688136 | tf_op jit(solution)/shard_map/ppermute | solution.py:679
  62.2 0.7 copy-start
  62.2 0.7 copy-start.1

commit v2 on v1

v2 whole, which is shorter than its diff:
```python
import jax
import jax.numpy as jnp
from jax import lax
from jax.experimental import pallas as pl
from jax.experimental.pallas import tpu as pltpu
from jax.sharding import PartitionSpec as P

HEAD_DIM = 128
ROWS = 224
SPAN = 112
GROUP = 8
ZK = 896
COLS = 1024
SCALE = HEAD_DIM**-0.5
SCALE2 = SCALE * 1.4426950408889634
FILL = -1e30
MESH = pl.DeviceIdType.MESH
F32 = jnp.float32
BF16 = jnp.bfloat16


def dot_nn(a, b):
    return lax.dot_general(a, b, (((1,), (0,)), ((), ())), preferred_element_type=F32)


def dot_nt(a, b):
    return lax.dot_general(a, b, (((1,), (1,)), ((), ())), preferred_element_type=F32)


def dot_tn(a, b):
    return lax.dot_general(a, b, (((0,), (0,)), ((), ())), preferred_element_type=F32)


class Here:
    def __init__(self):
        d = lax.axis_index("dc")
        t = lax.axis_index("tp")
        self.d, self.t = d, t
        self.c = lax.rem(d, 2)
        self.x = lax.rem(lax.div(d, 2), 2)
        self.z = lax.div(d, 4)
        self.h = lax.rem(t, 2)
        self.y = lax.div(t, 2)

    def by_dc(self, z, x):
        return ((z * 2 + x) * 2 + self.c, self.t)

    def by_tp(self, y, h):
        return (self.d, y * 2 + h)

    def sibling(self):
        return ((self.z * 2 + self.x) * 2 + (1 - self.c), self.t)


def around(a):
    return lax.rem(a + 1, 4), lax.rem(a + 3, 4), lax.rem(a + 2, 4)


def meet(devices):
    barrier = pltpu.get_barrier_semaphore()
    for device in devices:
        pl.semaphore_signal(barrier, inc=1, device_id=device, device_id_type=MESH)
    pl.semaphore_wait(barrier, len(devices))


class Gather:
    def __init__(self, view, a, b, dev, ssem, rsem, rows, cross=0):
        up, dn, far = around(a)
        o = 1 - b
        self.view, self.ssem, self.rsem = view, ssem, rsem
        self.count = 12 if cross else 9
        half, some = rows // 2, (rows - cross) // 2
        whole, low, high = (0, rows), (0, half), (half, half)
        rest, first, second = (cross, rows - cross), (cross, some), (cross + some, some)
        over = (0, cross)
        self.out = [
            (a, b, whole, dev(a, o)),
            (a, b, whole, dev(up, b)),
            (a, b, whole, dev(dn, b)),
            (a, o, rest, dev(up, b)),
            (a, o, rest, dev(dn, b)),
            (dn, b, low, dev(up, b)),
            (up, b, high, dev(dn, b)),
            (dn, o, first, dev(up, b)),
            (up, o, second, dev(dn, b)),
            (dn, b, over, dev(a, o)),
            (up, b, over, dev(a, o)),
            (far, b, over, dev(a, o)),
        ]
        self.into = [
            (a, o, whole),
            (dn, b, whole),
            (up, b, whole),
            (dn, o, rest),
            (up, o, rest),
            (far, b, low),
            (far, b, high),
            (far, o, first),
            (far, o, second),
            (dn, o, over),
            (up, o, over),
            (far, o, over),
        ]

    def copy(self, i, part):
        ref = self.view(*part)
        return pltpu.make_async_remote_copy(
            ref, ref, self.ssem.at[i], self.rsem.at[i],
            device_id=self.out[i][3], device_id_type=MESH,
        )

    def send(self, *order):
        for i in order:
            if i < self.count:
                a, b, (first, rows), _ = self.out[i]
                self.copy(i, (a, b, first, rows)).start()

    def got(self, *order):
        for i in order:
            if i < self.count:
                a, b, (first, rows) = self.into[i]
                self.copy(i, (a, b, first, rows)).wait_recv()

    def start(self):
        self.send(1, 2, 0)

    def pair(self):
        self.got(0)
        self.send(3, 4)

    def near(self):
        self.got(1)
        self.send(5, 9)
        self.got(2)
        self.send(6, 10)

    def near_pair(self):
        self.got(3)
        self.send(7)
        self.got(4)
        self.send(8)

    def far(self):
        self.got(5)
        self.send(11)
        self.got(6)

    def near_over(self):
        self.got(9, 10)

    def far_pair(self):
        self.got(7, 8, 11)

    def drain(self):
        for i in range(self.count):
            a, b, (first, rows), _ = self.out[i]
            self.copy(i, (a, b, first, rows)).wait_send()


class Sibling:
    def __init__(self, view, here, ssem, rsem):
        up, dn, far = around(here.z)
        x, o = here.x, 1 - here.x
        self.here, self.view, self.ssem, self.rsem = here, view, ssem, rsem
        self.blocks = [
            (here.z, x), (here.z, o), (dn, x), (up, x), (dn, o), (up, o), (far, x), (far, o),
        ]

    def sent(self, i, core):
        z, x = self.blocks[i]
        ref = self.view(z, x, core)
        return pltpu.make_async_remote_copy(
            ref, ref, self.ssem.at[i], self.rsem.at[i],
            device_id=self.here.sibling(), device_id_type=MESH,
        )

    def start(self, *order):
        for i in order:
            self.sent(i, self.here.c).start()

    def got(self, *order):
        for i in order:
            self.sent(i, 1 - self.here.c).wait_recv()

    def drain(self):
        for i in range(8):
            self.sent(i, self.here.c).wait_send()


class Reduce:
    def __init__(self, emit, a, b, dev, sbuf, rbuf, ssem, rsem):
        up, dn, far = around(a)
        self.emit, self.b, self.sbuf, self.rbuf, self.ssem, self.rsem = emit, b, sbuf, rbuf, ssem, rsem
        u, d, p = dev(up, b), dev(dn, b), dev(a, 1 - b)
        self.devices = [u, d, u, d, u, d, p]

    def copy(self, i):
        return pltpu.make_async_remote_copy(
            self.sbuf.at[i], self.rbuf.at[i], self.ssem.at[i], self.rsem.at[i],
            device_id=self.devices[i], device_id_type=MESH,
        )

    def send(self, i, which, b, adds=()):
        self.emit(self.sbuf.at[i], which, b, [self.rbuf.at[j] for j in adds])
        self.copy(i).start()

    def far(self):
        self.send(0, "far", 0)
        self.send(1, "far", 1)

    def near(self):
        self.send(2, "up", 1)
        self.send(3, "dn", 0)

    def comb(self):
        self.copy(0).wait_recv()
        self.send(4, "up", 0, [0])
        self.copy(1).wait_recv()
        self.send(5, "dn", 1, [1])

    def pair(self):
        for i in (2, 3, 4, 5):
            self.copy(i).wait_recv()
        o = 1 - self.b
        self.send(6, "own", o, [4 + o, 3 - o])

    def final(self, out):
        self.copy(6).wait_recv()
        b = self.b
        self.emit(out, "own", b, [self.rbuf.at[j] for j in (4 + b, 3 - b, 6)])

    def drain(self):
        for i in range(7):
            self.copy(i).wait_send()


def write_bias(bias, place_ref, length_ref, here):
    row = lax.broadcasted_iota(jnp.int32, (ROWS, 1), 0)
    first, second = place_ref[2 * here.d], place_ref[2 * here.d + 1]
    pos = row + jnp.where(row < SPAN, first * SPAN, second * SPAN - SPAN)
    low = jnp.zeros((ROWS, 1), jnp.int32)
    bound = length_ref[0]
    for i in range(1, 4):
        low = jnp.where(pos >= bound, bound, low)
        bound = bound + length_ref[i]

    def fill(z, carry):
        lane = lax.broadcasted_iota(jnp.int32, (1, ZK), 1)
        key = jnp.zeros((1, ZK), jnp.int32)
        for i in range(8):
            begin = place_ref[8 * z + i] * SPAN - i * SPAN
            key = jnp.where(lane >= i * SPAN, lane + begin, key)
        bias[z] = jnp.where((key >= low) & (key <= pos), 0.0, FILL)
        return carry

    lax.fori_loop(0, 4, fill, 0)


def split_heads(dst, src):
    for head in range(GROUP):
        dst[head] = src[:, head * HEAD_DIM : (head + 1) * HEAD_DIM]


def keys_of(kv, which, z):
    return kv[which, pl.ds(4 * z, 4)].reshape(ZK, HEAD_DIM)


def shifted(z):
    return jnp.where(z == 0, 1, jnp.where(z == 1, 3, jnp.where(z == 2, 2, 0)))


def layer_kernel(
    q_ref, k_ref, v_ref, w_ref, g_ref, place_ref, length_ref,
    out_ref, dq_ref, dk_ref, dv_ref, gw_ref,
    kv, gbuf, wbuf, attall, gcol, q_s, do_s, qt_s, dot_s, bias, top, total, oacc, hacc,
    kt, vt, keep, sib_out, sib_in, c_out, c_in, d_out, d_in, d_final, gacc,
    wsem, kv_s, kv_r, kvsib_s, kvsib_r, g_s, g_r, per_s, per_r, att_s, att_r, sib_s, sib_r,
    col_s, col_r, c_s, c_r, x_s, x_r, d_s, d_r,
):
    here = Here()
    zu, zd, zf = around(here.z)
    yu, yd, yf = around(here.y)
    h, o = here.h, 1 - here.h
    half = COLS // 2

    def load_w(j):
        return pltpu.make_async_copy(w_ref.at[:, pl.ds(j * COLS, COLS)], wbuf.at[j], wsem.at[j])

    for j in range(8):
        load_w(j).start()

    def kv_view(z, x, first, rows):
        return kv.at[:, (z * 2 + x) * 2 + here.c, pl.ds(first, rows)]

    def att_view(z, x, first, rows):
        return attall.at[(z * 2 + x) * 2 + here.c, pl.ds(first, rows)]

    kvg = Gather(kv_view, here.z, here.x, here.by_dc, kv_s, kv_r, ROWS)
    kvsib = Sibling(lambda z, x, core: kv.at[:, (z * 2 + x) * 2 + core], here, kvsib_s, kvsib_r)
    gg = Gather(
        lambda y, h, first, rows: gbuf.at[y * 2 + h, pl.ds(first, rows)],
        here.y, h, here.by_tp, g_s, g_r, ROWS, 64,
    )
    ag = Gather(att_view, here.z, here.x, here.by_dc, att_s, att_r, ROWS)
    sib = Sibling(lambda z, x, core: attall.at[(z * 2 + x) * 2 + core], here, sib_s, sib_r)
    cg = Gather(
        lambda y, h, first, rows: gcol.at[y * 2 + h, pl.ds(first, rows)],
        here.y, h, here.by_tp, col_s, col_r, 2 * ROWS, 128,
    )

    to_y = lax.rem(shifted(here.y) - here.z + 4, 4)
    from_z = lax.rem(shifted(here.z) - here.y + 4, 4)

    def to_chip(core):
        return ((here.y * 2 + h) * 2 + core, to_y * 2 + here.x)

    def from_chip(core):
        return ((from_z * 2 + h) * 2 + core, here.z * 2 + here.x)

    def handed(i):
        core = here.c if i == 0 else 1 - here.c
        cols = pl.ds(pl.multiple_of(core * half, half), half)
        rows = pl.ds(pl.multiple_of(here.c * ROWS, ROWS), ROWS)
        return pltpu.make_async_remote_copy(
            g_ref.at[:, cols], gcol.at[to_y * 2 + here.x, rows], per_s.at[i], per_r.at[i],
            device_id=to_chip(core), device_id_type=MESH,
        )

    def taken(i):
        core = here.c if i == 0 else 1 - here.c
        rows = pl.ds(pl.multiple_of(core * ROWS, ROWS), ROWS)
        ref = gcol.at[here.t, rows]
        pltpu.make_async_remote_copy(
            ref, ref, per_s.at[i], per_r.at[i], device_id=from_chip(core), device_id_type=MESH
        ).wait_recv()

    kv[0, here.d] = k_ref[...]
    kv[1, here.d] = v_ref[...]
    gbuf[here.t] = g_ref[...]
    meet(
        [
            here.by_dc(zu, here.x), here.by_dc(zd, here.x), here.by_dc(here.z, 1 - here.x), here.sibling(),
            here.by_tp(yu, h), here.by_tp(yd, h), here.by_tp(here.y, o),
            from_chip(here.c), from_chip(1 - here.c),
        ]
    )
    kvg.start()
    kvsib.start(0)
    gg.start()
    handed(0).start()
    handed(1).start()
    split_heads(q_s, q_ref)
    write_bias(bias, place_ref, length_ref, here)
    top[...] = jnp.full(top.shape, FILL, F32)
    total[...] = jnp.zeros(total.shape, F32)
    oacc[...] = jnp.zeros(oacc.shape, F32)
    hacc[...] = jnp.zeros(hacc.shape, F32)

    def scores(z, g):
        q = q_s[pl.ds(2 * g, 2)].reshape(2 * ROWS, HEAD_DIM)
        s = dot_nt(q, keys_of(kv, 0, z)) * SCALE2
        s = s.reshape(2, ROWS, ZK) + bias[z][None]
        return s.reshape(2 * ROWS, ZK)

    def attend(z):
        def step(g, carry):
            s = scores(z, g)
            high = s[:, :128]
            for j in range(1, ZK // 128):
                high = jnp.maximum(high, s[:, j * 128 : (j + 1) * 128])
            old = top[g]
            new = jnp.maximum(old, jnp.max(high, axis=1, keepdims=True))
            p = jnp.exp2(s - new[:, :1])
            alpha = jnp.exp2(old - new)
            part = total[g] * alpha
            for j in range(ZK // 128):
                part = part + p[:, j * 128 : (j + 1) * 128]
            total[g] = part
            top[g] = new
            oacc[g] = oacc[g] * alpha + dot_nn(p.astype(BF16), keys_of(kv, 1, z))
            return carry

        lax.fori_loop(0, 4, step, 0)

    def head_grads(y, h):
        slot = y * 2 + h

        def tile(n, carry):
            rows = pl.ds(pl.multiple_of(n * 256, 256), 256)
            hacc[rows, :] += dot_nt(wbuf[slot, rows, :], gbuf[slot])
            return carry

        lax.fori_loop(0, 4, tile, 0)

    def out_part(dst, which, h, adds):
        slot = {"far": yf, "up": yu, "dn": yd, "own": here.y}[which] * 2 + h

        def tile(n, carry):
            cols = pl.ds(pl.multiple_of(n * 256, 256), 256)
            acc = dot_nn(attall[here.d], wbuf[slot, :, cols])
            for add in adds:
                acc = acc + add[:, cols].astype(F32)
            dst[:, cols] = acc.astype(BF16)
            return carry

        lax.fori_loop(0, 4, tile, 0)

    def kv_part(dst, which, x, adds):
        r = {"far": 0, "dn": 1, "up": 2, "own": 3}[which]
        acc = keep[r, x] + sib_in[r, x].astype(F32)
        for add in adds:
            acc = acc + add[...].astype(F32)
        dst[...] = acc.astype(BF16)

    c_red = Reduce(out_part, here.y, h, here.by_tp, c_out, c_in, c_s, c_r)
    d_red = Reduce(kv_part, here.z, here.x, here.by_dc, d_out, d_in, d_s, d_r)

    def sib_sum(r):
        return pltpu.make_async_remote_copy(
            sib_out.at[r], sib_in.at[r], x_s.at[r], x_r.at[r],
            device_id=here.sibling(), device_id_type=MESH,
        )

    def plane(r, z):
        kt[...] = jnp.zeros(kt.shape, F32)
        vt[...] = jnp.zeros(vt.shape, F32)

        def step(g, carry):
            k, v = keys_of(kv, 0, z), keys_of(kv, 1, z)
            do = do_s[pl.ds(2 * g, 2)].reshape(2 * ROWS, HEAD_DIM)
            p = jnp.exp2(scores(z, g) - top[g][:, :1])
            ds = (p * (dot_nt(do, v) - total[g][:, :1])).astype(BF16)
            oacc[g] += dot_nn(ds, k)
            kt[...] += dot_nn(qt_s[g], ds)
            vt[...] += dot_nn(dot_s[g], p.astype(BF16))
            return carry

        lax.fori_loop(0, 4, step, 0)
        dk = (kt[...] * SCALE).T.reshape(4, ROWS, HEAD_DIM)
        dv = vt[...].T.reshape(4, ROWS, HEAD_DIM)
        for x in range(2):
            mine = here.c == 0
            for which, value in ((0, dk), (1, dv)):
                even, odd = value[2 * x], value[2 * x + 1]
                keep[r, x, which] = jnp.where(mine, even, odd)
                sib_out[r, x, which] = jnp.where(mine, odd, even).astype(BF16)
        sib_sum(r).start()

    def weight_part(y, h):
        chip = lax.rem(shifted(here.z) - y + 4, 4) * 2 + h
        right = gcol[y * 2 + h]

        def tile(n, carry):
            cols = pl.ds(pl.multiple_of(n * 256, 256), 256)
            left = attall[pl.ds(2 * chip, 2), :, cols].reshape(2 * ROWS, 256)
            gacc[cols, :] += dot_tn(left, right)
            return carry

        lax.fori_loop(0, 4, tile, 0)

    def finish_attention():
        for g in range(4):
            whole = jnp.broadcast_to(jnp.sum(total[g], axis=1, keepdims=True), (2 * ROWS, 128))
            top[g] = top[g] + jnp.log2(whole)
            value = (oacc[g] / whole).astype(BF16)
            for j in range(2):
                head = 2 * g + j
                attall[here.d, :, head * HEAD_DIM : (head + 1) * HEAD_DIM] = value[j * ROWS : (j + 1) * ROWS]

    def prepare_backward():
        for g in range(4):
            for j in range(2):
                head = 2 * g + j
                grads = hacc[pl.ds(head * HEAD_DIM, HEAD_DIM), :]
                dot_s[g, :, j * ROWS : (j + 1) * ROWS] = grads.astype(BF16)
                do = grads.T.astype(BF16)
                do_s[head] = do
                a = attall[here.d, :, head * HEAD_DIM : (head + 1) * HEAD_DIM].astype(F32)
                total[g, pl.ds(j * ROWS, ROWS)] = jnp.broadcast_to(
                    jnp.sum(a * do.astype(F32), axis=1, keepdims=True), (ROWS, 128)
                )
            qt_s[g] = q_s[pl.ds(2 * g, 2)].reshape(2 * ROWS, HEAD_DIM).T
        oacc[...] = jnp.zeros(oacc.shape, F32)

    def write_grad_queries():
        for g in range(4):
            value = (oacc[g] * SCALE).astype(BF16)
            for j in range(2):
                head = 2 * g + j
                dq_ref[:, head * HEAD_DIM : (head + 1) * HEAD_DIM] = value[j * ROWS : (j + 1) * ROWS]

    def write_grad_keys_values():
        d_red.final(d_final)
        dk_ref[...] = d_final[0]
        dv_ref[...] = d_final[1]

    def wait_w():
        for j in range(8):
            load_w(j).wait()

    def take():
        taken(0)
        taken(1)

    def clear():
        gacc[...] = jnp.zeros(gacc.shape, F32)

    def summed(*order):
        for r in order:
            sib_sum(r).wait_recv()

    def write_grad_weight():
        gw_ref[...] = gacc[...].astype(BF16)

    def drain():
        for group in (kvg, kvsib, gg, ag, sib, cg, c_red, d_red):
            group.drain()
        for i in range(2):
            handed(i).wait_send()
        for r in range(4):
            sib_sum(r).wait_send()

    steps = [
        (kvg.pair,),
        (kvsib.start, 1),
        (kvg.near,),
        (kvsib.start, 2, 3),
        (kvsib.got, 0, 1),
        (attend, here.z),
        (kvg.near_pair,),
        (kvsib.start, 4, 5),
        (kvg.far,),
        (kvsib.start, 6),
        (kvsib.got, 2, 4),
        (attend, zd),
        (kvg.far_pair,),
        (kvsib.start, 7),
        (kvsib.got, 3, 5),
        (attend, zu),
        (gg.near,),
        (gg.pair,),
        (kvsib.got, 6, 7),
        (attend, zf),
        (finish_attention,),
        (ag.start,),
        (sib.start, 0),
        (wait_w,),
        (c_red.far,),
        (gg.near_pair,),
        (c_red.near,),
        (gg.far,),
        (take,),
        (cg.start,),
        (head_grads, here.y, h),
        (head_grads, here.y, o),
        (head_grads, yd, h),
        (head_grads, yu, h),
        (ag.pair,),
        (sib.start, 1),
        (ag.near,),
        (sib.start, 2, 3),
        (gg.near_over,),
        (head_grads, yd, o),
        (head_grads, yu, o),
        (head_grads, yf, h),
        (gg.far_pair,),
        (head_grads, yf, o),
        (prepare_backward,),
        (c_red.comb,),
        (plane, 0, zf),
        (ag.near_pair,),
        (sib.start, 4, 5),
        (cg.near,),
        (cg.pair,),
        (plane, 1, zd),
        (summed, 0),
        (d_red.far,),
        (ag.far,),
        (sib.start, 6),
        (plane, 2, zu),
        (ag.far_pair,),
        (sib.start, 7),
        (summed, 1, 2),
        (d_red.near,),
        (cg.near_pair,),
        (plane, 3, here.z),
        (d_red.comb,),
        (c_red.pair,),
        (write_grad_queries,),
        (summed, 3),
        (d_red.pair,),
        (sib.got, *range(8)),
        (clear,),
        (cg.far,),
        (weight_part, here.y, h),
        (weight_part, here.y, o),
        (weight_part, yd, h),
        (weight_part, yu, h),
        (write_grad_keys_values,),
        (cg.near_over,),
        (weight_part, yd, o),
        (weight_part, yu, o),
        (weight_part, yf, h),
        (c_red.final, out_ref),
        (cg.far_pair,),
        (weight_part, yf, o),
        (write_grad_weight,),
        (drain,),
    ]
    for step, *given in steps:
        step(*given)


def vmem():
    return pl.BlockSpec(memory_space=pltpu.VMEM)


def smem():
    return pl.BlockSpec(memory_space=pltpu.SMEM)


def anywhere():
    return pl.BlockSpec(memory_space=pl.ANY)


def dma(n):
    return pltpu.SemaphoreType.DMA((n,))


def result_shapes():
    shape = jax.ShapeDtypeStruct
    return (
        shape((ROWS, COLS), BF16),
        shape((ROWS, COLS), BF16),
        shape((ROWS, HEAD_DIM), BF16),
        shape((ROWS, HEAD_DIM), BF16),
        shape((COLS, COLS // 2), BF16),
    )


def layer(q, k, v, w, g, place, length):
    return pl.pallas_call(
        layer_kernel,
        out_shape=result_shapes(),
        in_specs=[vmem(), vmem(), vmem(), anywhere(), vmem(), smem(), smem()],
        out_specs=(vmem(),) * 5,
        scratch_shapes=[
            pltpu.VMEM((2, 16, ROWS, HEAD_DIM), BF16),
            pltpu.VMEM((8, ROWS, COLS), BF16),
            pltpu.VMEM((8, COLS, COLS), BF16),
            pltpu.VMEM((16, ROWS, COLS), BF16),
            pltpu.VMEM((8, 2 * ROWS, COLS // 2), BF16),
            pltpu.VMEM((GROUP, ROWS, HEAD_DIM), BF16),
            pltpu.VMEM((GROUP, ROWS, HEAD_DIM), BF16),
            pltpu.VMEM((4, HEAD_DIM, 2 * ROWS), BF16),
            pltpu.VMEM((4, HEAD_DIM, 2 * ROWS), BF16),
            pltpu.VMEM((4, ROWS, ZK), F32),
            pltpu.VMEM((4, 2 * ROWS, 128), F32),
            pltpu.VMEM((4, 2 * ROWS, 128), F32),
            pltpu.VMEM((4, 2 * ROWS, 128), F32),
            pltpu.VMEM((COLS, ROWS), F32),
            pltpu.VMEM((HEAD_DIM, ZK), F32),
            pltpu.VMEM((HEAD_DIM, ZK), F32),
            pltpu.VMEM((4, 2, 2, ROWS, HEAD_DIM), F32),
            pltpu.VMEM((4, 2, 2, ROWS, HEAD_DIM), BF16),
            pltpu.VMEM((4, 2, 2, ROWS, HEAD_DIM), BF16),
            pltpu.VMEM((7, ROWS, COLS), BF16),
            pltpu.VMEM((7, ROWS, COLS), BF16),
            pltpu.VMEM((7, 2, ROWS, HEAD_DIM), BF16),
            pltpu.VMEM((7, 2, ROWS, HEAD_DIM), BF16),
            pltpu.VMEM((2, ROWS, HEAD_DIM), BF16),
            pltpu.VMEM((COLS, COLS // 2), F32),
            dma(8), dma(9), dma(9), dma(8), dma(8), dma(12), dma(12), dma(2), dma(2),
            dma(9), dma(9), dma(8), dma(8), dma(12), dma(12), dma(7), dma(7), dma(4), dma(4),
            dma(7), dma(7),
        ],
        compiler_params=pltpu.CompilerParams(
            collective_id=0, has_side_effects=True, vmem_limit_bytes=63 * 2**20
        ),
        cost_estimate=pl.CostEstimate(flops=24 * 10**9, bytes_accessed=24 * 10**6, transcendentals=12 * 10**6),
    )(q, k, v, w, g, place, length)


def hand_over_kernel(*refs):
    for source, result in zip(refs[:5], refs[5:]):
        result[...] = source[...]


def hand_over(*arrays):
    return pl.pallas_call(
        hand_over_kernel,
        out_shape=result_shapes(),
        in_specs=[vmem()] * 5,
        out_specs=(vmem(),) * 5,
    )(*arrays)


def on_device(q, k, v, w, g, place, length):
    return hand_over(*layer(q, k, v, w, g, place, length))


def solution(mesh):
    in_specs = (P("dc", "tp"), P("dc", "tp"), P("dc", "tp"), P("tp", None), P("dc", "tp"), P(), P())
    out_specs = (P("dc", "tp"), P("dc", "tp"), P("dc", "tp"), P("dc", "tp"), P("tp", "dc"))
    return jax.shard_map(
        on_device, mesh=mesh, in_specs=in_specs, out_specs=out_specs, check_vma=False
    )
```

time: 151 us -> 140 us (0.927)
  local copies, waits for them, and re-layouts: 10.6 us -> 0 us
  Pallas kernels: 137 us -> 139 us
    unnamed x9 -> x0, local copies, waits for them, and re-layouts: 9.52 us -> none
  transfers between devices with their start and end apart: 2 -> 0, of which waited for: 0 -> 0; matrix products, arithmetic and copies ran while one was open for 0% -> 0% of each run, Pallas kernels for 40% -> 0%
where the time goes in v2:
time: 140 us
  Pallas kernels  139 us (99%)
    pallas_call x1, Pallas kernels, layer(): pl.pallas_call(layer_kernel, out_shape=result_shapes(), in_specs=[vmem(),...  136 us
    pallas_call x1, Pallas kernels, hand_over(): pl.pallas_call(hand_over_kernel, out_shape=result_shapes(), in_specs=[vme...  2.9 us

profile of v2, /device:TPU:0, one launch (start us, length us, event | category | flops | bytes accessed | tf_op | source)
XLA Modules:
  0.0 139.5 jit_solution(5889750400659461192)
XLA Ops:
  0.6 136.0 %shard_map.110 = (bf16[224,1024]{1,0:T(8,128)(2,1)}, bf16[224,1024]{1,0:T(8,128)(2,1)}, bf16[224,128]{1,0:T(8,128)(2,1)}, bf16[224,128]{1,0:T(8,128)(2,1)}, bf16[1024,512]{1,0:T(8,128)(2,1)}) custom-call(bf16[224,1024]{1,0:T(8,128)(2,1)} %q_ref.1, bf16[224,128]{1,0:T(8,128)(2,1)} %k_ref.1, bf16[224,128]{1,0:T(8,128)(2,1)} %v_ref.1, ...), custom_call_target="tpu_custom_call" | custom-call | flops 24000000000 | bytes 24000000 | tf_op jit(solution)/shard_map/pallas_call | solution.py:642
  136.6 2.9 %shard_map.111 = (bf16[224,1024]{1,0:T(8,128)(2,1)}, bf16[224,1024]{1,0:T(8,128)(2,1)}, bf16[224,128]{1,0:T(8,128)(2,1)}, bf16[224,128]{1,0:T(8,128)(2,1)}, bf16[1024,512]{1,0:T(8,128)(2,1)}) custom-call(bf16[224,1024]{1,0:T(8,128)(2,1)} %get-tuple-element.10.refs_0_, bf16[224,1024]{1,0:T(8,128)(2,1)} %get-tuple-element.11.refs_1_, ...), custom_call_target="tpu_custom_call" | custom-call | tf_op jit(solution)/shard_map/pallas_call | solution.py:690

commit v3 on v2

--- a/solution.py
+++ b/solution.py
@@ -121,8 +121,11 @@
                 a, b, (first, rows) = self.into[i]
                 self.copy(i, (a, b, first, rows)).wait_recv()
 
-    def start(self):
-        self.send(1, 2, 0)
+    def start_pair(self):
+        self.send(0)
+
+    def start_near(self):
+        self.send(1, 2)
 
     def pair(self):
         self.got(0)
@@ -204,19 +207,37 @@
         self.emit(self.sbuf.at[i], which, b, [self.rbuf.at[j] for j in adds])
         self.copy(i).start()
 
+    def far_up(self):
+        self.send(0, "far", 0)
+
+    def far_dn(self):
+        self.send(1, "far", 1)
+
     def far(self):
-        self.send(0, "far", 0)
-        self.send(1, "far", 1)
+        self.far_up()
+        self.far_dn()
+
+    def near_up(self):
+        self.send(2, "up", 1)
+
+    def near_dn(self):
+        self.send(3, "dn", 0)
 
     def near(self):
-        self.send(2, "up", 1)
-        self.send(3, "dn", 0)
-
-    def comb(self):
+        self.near_up()
+        self.near_dn()
+
+    def comb_up(self):
         self.copy(0).wait_recv()
         self.send(4, "up", 0, [0])
+
+    def comb_dn(self):
         self.copy(1).wait_recv()
         self.send(5, "dn", 1, [1])
+
+    def comb(self):
+        self.comb_up()
+        self.comb_dn()
 
     def pair(self):
         for i in (2, 3, 4, 5):
@@ -299,13 +320,13 @@
     kvsib = Sibling(lambda z, x, core: kv.at[:, (z * 2 + x) * 2 + core], here, kvsib_s, kvsib_r)
     gg = Gather(
         lambda y, h, first, rows: gbuf.at[y * 2 + h, pl.ds(first, rows)],
-        here.y, h, here.by_tp, g_s, g_r, ROWS, 64,
+        here.y, h, here.by_tp, g_s, g_r, ROWS, 0,
     )
     ag = Gather(att_view, here.z, here.x, here.by_dc, att_s, att_r, ROWS)
     sib = Sibling(lambda z, x, core: attall.at[(z * 2 + x) * 2 + core], here, sib_s, sib_r)
     cg = Gather(
         lambda y, h, first, rows: gcol.at[y * 2 + h, pl.ds(first, rows)],
-        here.y, h, here.by_tp, col_s, col_r, 2 * ROWS, 128,
+        here.y, h, here.by_tp, col_s, col_r, 2 * ROWS, 0,
     )
 
     to_y = lax.rem(shifted(here.y) - here.z + 4, 4)
@@ -344,11 +365,10 @@
             from_chip(here.c), from_chip(1 - here.c),
         ]
     )
-    kvg.start()
+    kvg.start_pair()
+    kvg.start_near()
     kvsib.start(0)
-    gg.start()
-    handed(0).start()
-    handed(1).start()
+    gg.start_near()
     split_heads(q_s, q_ref)
     write_bias(bias, place_ref, length_ref, here)
     top[...] = jnp.full(top.shape, FILL, F32)
@@ -362,22 +382,32 @@
         s = s.reshape(2, ROWS, ZK) + bias[z][None]
         return s.reshape(2 * ROWS, ZK)
 
+    def maxima(z):
+        def step(g, carry):
+            s = scores(z, g)
+            high = top[g]
+            for j in range(ZK // 128):
+                high = jnp.maximum(high, s[:, j * 128 : (j + 1) * 128])
+            top[g] = high
+            return carry
+
+        lax.fori_loop(0, 4, step, 0)
+
+    def spread():
+        def step(g, carry):
+            top[g] = jnp.broadcast_to(jnp.max(top[g], axis=1, keepdims=True), (2 * ROWS, 128))
+            return carry
+
+        lax.fori_loop(0, 4, step, 0)
+
     def attend(z):
         def step(g, carry):
-            s = scores(z, g)
-            high = s[:, :128]
-            for j in range(1, ZK // 128):
-                high = jnp.maximum(high, s[:, j * 128 : (j + 1) * 128])
-            old = top[g]
-            new = jnp.maximum(old, jnp.max(high, axis=1, keepdims=True))
-            p = jnp.exp2(s - new[:, :1])
-            alpha = jnp.exp2(old - new)
-            part = total[g] * alpha
+            p = jnp.exp2(scores(z, g) - top[g][:, :1])
+            part = total[g]
             for j in range(ZK // 128):
                 part = part + p[:, j * 128 : (j + 1) * 128]
             total[g] = part
-            top[g] = new
-            oacc[g] = oacc[g] * alpha + dot_nn(p.astype(BF16), keys_of(kv, 1, z))
+            oacc[g] += dot_nn(p.astype(BF16), keys_of(kv, 1, z))
             return carry
 
         lax.fori_loop(0, 4, step, 0)
@@ -421,10 +451,7 @@
             device_id=here.sibling(), device_id_type=MESH,
         )
 
-    def plane(r, z):
-        kt[...] = jnp.zeros(kt.shape, F32)
-        vt[...] = jnp.zeros(vt.shape, F32)
-
+    def plane(z, first):
         def step(g, carry):
             k, v = keys_of(kv, 0, z), keys_of(kv, 1, z)
             do = do_s[pl.ds(2 * g, 2)].reshape(2 * ROWS, HEAD_DIM)
@@ -435,7 +462,15 @@
             vt[...] += dot_nn(dot_s[g], p.astype(BF16))
             return carry
 
-        lax.fori_loop(0, 4, step, 0)
+        lax.fori_loop(first, first + 2, step, 0)
+
+    def plane_a(r, z):
+        kt[...] = jnp.zeros(kt.shape, F32)
+        vt[...] = jnp.zeros(vt.shape, F32)
+        plane(z, 0)
+
+    def plane_b(r, z):
+        plane(z, 2)
         dk = (kt[...] * SCALE).T.reshape(4, ROWS, HEAD_DIM)
         dv = vt[...].T.reshape(4, ROWS, HEAD_DIM)
         for x in range(2):
@@ -498,6 +533,10 @@
         for j in range(8):
             load_w(j).wait()
 
+    def hand():
+        handed(0).start()
+        handed(1).start()
+
     def take():
         taken(0)
         taken(1)
@@ -522,86 +561,103 @@
 
     steps = [
         (kvg.pair,),
+        (gg.start_pair,),
+        (kvg.near,),
         (kvsib.start, 1),
-        (kvg.near,),
         (kvsib.start, 2, 3),
-        (kvsib.got, 0, 1),
-        (attend, here.z),
         (kvg.near_pair,),
         (kvsib.start, 4, 5),
+        (hand,),
+        (kvsib.got, 2, 4),
+        (kvsib.got, 3, 5),
+        (maxima, zd),
+        (wait_w,),
+        (kvsib.got, 0, 1),
+        (gg.near,),
+        (head_grads, yu, h),
         (kvg.far,),
         (kvsib.start, 6),
-        (kvsib.got, 2, 4),
+        (head_grads, yd, h),
+        (kvg.far_pair,),
+        (maxima, zu),
+        (kvsib.start, 7),
+        (take,),
+        (gg.pair,),
+        (head_grads, here.y, o),
+        (kvsib.got, 6, 7),
+        (maxima, zf),
+        (maxima, here.z),
+        (cg.start_near,),
+        (gg.far,),
+        (spread,),
+        (gg.near_over,),
+        (attend, zu),
+        (gg.near_pair,),
         (attend, zd),
-        (kvg.far_pair,),
-        (kvsib.start, 7),
-        (kvsib.got, 3, 5),
-        (attend, zu),
-        (gg.near,),
-        (gg.pair,),
-        (kvsib.got, 6, 7),
         (attend, zf),
+        (attend, here.z),
         (finish_attention,),
-        (ag.start,),
-        (sib.start, 0),
-        (wait_w,),
-        (c_red.far,),
-        (gg.near_pair,),
-        (c_red.near,),
-        (gg.far,),
-        (take,),
-        (cg.start,),
-        (head_grads, here.y, h),
-        (head_grads, here.y, o),
-        (head_grads, yd, h),
-        (head_grads, yu, h),
-        (ag.pair,),
-        (sib.start, 1),
-        (ag.near,),
-        (sib.start, 2, 3),
-        (gg.near_over,),
+        (c_red.far_up,),
+        (ag.start_pair,),
+        (c_red.far_dn,),
         (head_grads, yd, o),
+        (ag.start_near,),
         (head_grads, yu, o),
         (head_grads, yf, h),
         (gg.far_pair,),
+        (cg.start_pair,),
         (head_grads, yf, o),
+        (c_red.near_up,),
+        (clear,),
+        (head_grads, here.y, h),
+        (c_red.near_dn,),
         (prepare_backward,),
-        (c_red.comb,),
-        (plane, 0, zf),
+        (c_red.comb_dn,),
+        (ag.near,),
+        (plane_a, 0, zf),
+        (ag.pair,),
+        (c_red.comb_up,),
+        (sib.start, 0),
+        (plane_b, 0, zf),
+        (plane_a, 1, zd),
+        (plane_b, 1, zd),
+        (ag.far,),
+        (plane_a, 2, zu),
+        (plane_b, 2, zu),
+        (cg.near,),
+        (summed, 0),
         (ag.near_pair,),
+        (plane_a, 3, here.z),
+        (sib.start, 6),
+        (d_red.far,),
         (sib.start, 4, 5),
-        (cg.near,),
         (cg.pair,),
-        (plane, 1, zd),
-        (summed, 0),
-        (d_red.far,),
-        (ag.far,),
-        (sib.start, 6),
-        (plane, 2, zu),
+        (sib.start, 2, 3),
+        (summed, 2),
+        (c_red.pair,),
+        (cg.near_over,),
+        (sib.start, 1),
+        (plane_b, 3, here.z),
+        (cg.far,),
         (ag.far_pair,),
         (sib.start, 7),
-        (summed, 1, 2),
+        (write_grad_queries,),
+        (summed, 1),
         (d_red.near,),
+        (d_red.comb,),
+        (summed, 3),
+        (sib.got, 0, 1, 2, 3, 4, 5, 6, 7),
+        (weight_part, here.y, h),
+        (weight_part, yf, h),
+        (weight_part, yd, h),
+        (weight_part, here.y, o),
         (cg.near_pair,),
-        (plane, 3, here.z),
-        (d_red.comb,),
-        (c_red.pair,),
-        (write_grad_queries,),
-        (summed, 3),
+        (weight_part, yu, o),
         (d_red.pair,),
-        (sib.got, *range(8)),
-        (clear,),
-        (cg.far,),
-        (weight_part, here.y, h),
-        (weight_part, here.y, o),
-        (weight_part, yd, h),
         (weight_part, yu, h),
         (write_grad_keys_values,),
-        (cg.near_over,),
+        (c_red.final, out_ref),
         (weight_part, yd, o),
-        (weight_part, yu, o),
-        (weight_part, yf, h),
-        (c_red.final, out_ref),
         (cg.far_pair,),
         (weight_part, yf, o),
         (write_grad_weight,),

time: 140 us -> 123 us (0.88)
  Pallas kernels: 139 us -> 122 us
    pallas_call x1, Pallas kernels: 136 us -> 119 us  [layer(): pl.pallas_call(layer_kernel, out_shape=result_shapes(), in_specs=[vmem(),...]
where the time goes in v3:
time: 123 us
  Pallas kernels  122 us (99%)
    pallas_call x1, Pallas kernels, layer(): pl.pallas_call(layer_kernel, out_shape=result_shapes(), in_specs=[vmem(),...  119 us
    pallas_call x1, Pallas kernels, hand_over(): pl.pallas_call(hand_over_kernel, out_shape=result_shapes(), in_specs=[vme...  2.9 us

profile of v3, /device:TPU:0, one launch (start us, length us, event | category | flops | bytes accessed | tf_op | source)
XLA Modules:
  0.0 122.6 jit_solution(15350363576824341184)
XLA Ops:
  0.6 119.1 %shard_map.110 = (bf16[224,1024]{1,0:T(8,128)(2,1)}, bf16[224,1024]{1,0:T(8,128)(2,1)}, bf16[224,128]{1,0:T(8,128)(2,1)}, bf16[224,128]{1,0:T(8,128)(2,1)}, bf16[1024,512]{1,0:T(8,128)(2,1)}) custom-call(bf16[224,1024]{1,0:T(8,128)(2,1)} %q_ref.1, bf16[224,128]{1,0:T(8,128)(2,1)} %k_ref.1, bf16[224,128]{1,0:T(8,128)(2,1)} %v_ref.1, ...), custom_call_target="tpu_custom_call" | custom-call | flops 24000000000 | bytes 24000000 | tf_op jit(solution)/shard_map/pallas_call | solution.py:698
  119.7 2.9 %shard_map.111 = (bf16[224,1024]{1,0:T(8,128)(2,1)}, bf16[224,1024]{1,0:T(8,128)(2,1)}, bf16[224,128]{1,0:T(8,128)(2,1)}, bf16[224,128]{1,0:T(8,128)(2,1)}, bf16[1024,512]{1,0:T(8,128)(2,1)}) custom-call(bf16[224,1024]{1,0:T(8,128)(2,1)} %get-tuple-element.10.refs_0_, bf16[224,1024]{1,0:T(8,128)(2,1)} %get-tuple-element.11.refs_1_, ...), custom_call_target="tpu_custom_call" | custom-call | tf_op jit(solution)/shard_map/pallas_call | solution.py:746
